TPU v7x, 256 devices: a whole 4x4x8 slice. The times are simulated.
256 devices in a mesh: outer: 16 (over y_hi, z), inner: 16 (over x, y_lo, core).
Axes of the slice: x: 4, y: 4 (y_hi: 2, y_lo: 2; y = y_hi * 2 + y_lo), z: 8, core: 2. Of those that a mesh axis runs over, the one named last changes fastest.
Arguments:
- queries: bfloat16 [98304, 1024], P(('outer', 'inner')), may hold values from -80 to 80
- keys: bfloat16 [98304, 128], P(('outer', 'inner')), may hold values from -6 to 6
- values: bfloat16 [98304, 128], P(('outer', 'inner')), may hold values from -6 to 6
- saved_out: bfloat16 [98304, 1024], P(('outer', 'inner')), may hold values from -6 to 6
- saved_lse: float32 [98304, 8], P(('outer', 'inner')), may hold values from -20 to 250, as said below
- out_grad: bfloat16 [98304, 1024], P(('outer', 'inner')), may hold values from -24 to 24
- positions: int32 [98304], P(('outer', 'inner')), may hold values from 0 to 98303, as said below
Outputs:
- query_grad: bfloat16 [98304, 1024], P(('outer', 'inner'))
- key_grad: bfloat16 [98304, 128], P(('outer', 'inner'))
- value_grad: bfloat16 [98304, 128], P(('outer', 'inner'))
Inputs may be any that keep to these rules, and one draw needn't show every extreme that they name: saved_lse[t, h] is the log of the sum over the allowed u of exp(scores[h, t, u]), computed in float32. positions is a permutation of the token positions; the rows of each block are two runs of 192 consecutive ascending positions, the first starting at c * 192 and the second at (511 - c) * 192, where c differs from block to block.
All inputs are finite; a program needn't handle non-finite values.
Results may differ from a plain program's by a relative error of at most 0.006.
Values may be sent and summed in bfloat16 or wider, within the bound.
A program may use at most 128 MiB of HBM per device.

v0:
```python
import functools

import jax
import jax.numpy as jnp
import numpy as np
from jax import lax
from jax.experimental import pallas as pl
from jax.experimental.pallas import tpu as pltpu
from jax.sharding import PartitionSpec as P

F32 = jnp.float32
BF16 = jnp.bfloat16
REACH = 4
FAR = REACH + 1


def nn(a, b):
    return lax.dot_general(a, b, (((1,), (0,)), ((), ())), preferred_element_type=F32)


def nt(a, b):
    return lax.dot_general(a, b, (((1,), (1,)), ((), ())), preferred_element_type=F32)


def tn(a, b):
    return lax.dot_general(a, b, (((0,), (0,)), ((), ())), preferred_element_type=F32)


def kernel(
    n_outer,
    n_inner,
    q_hbm,
    k_hbm,
    v_hbm,
    o_hbm,
    lse_ref,
    g_hbm,
    pos_ref,
    dq_ref,
    dk_ref,
    dv_ref,
    qs,
    gs,
    yq,
    yg,
    o_vm,
    kv,
    mark,
    marks,
    dqt,
    own,
    terms,
    came,
    load_sem,
    kv_sem,
    mark_send,
    mark_recv,
    mark_load,
    put_sem,
    get_sem,
    term_send,
    term_recv,
):
    outer = lax.axis_index("outer")
    inner = lax.axis_index("inner")
    span, width = kv.shape[3], kv.shape[4]
    heads = q_hbm.shape[1] // width
    scale = width**-0.5
    exp_scale = float(np.log2(np.e)) * scale
    core = lax.rem(inner, 2)
    side = lax.rem(inner // 2, 2)

    def inner_at(step):
        return (outer, lax.rem(inner + n_inner + step, n_inner))

    def outer_at(step):
        return (lax.rem(outer + n_outer + step, n_outer), inner)

    loads = []
    for src, dst in ((k_hbm, 0), (v_hbm, 1)):
        for half in range(2):
            copy = pltpu.make_async_copy(
                src.at[pl.ds(half * span, span), :], kv.at[0, dst, half], kv_sem.at[dst, half]
            )
            copy.start()
            loads.append(copy)
    tiles = []
    for at, (src, dst) in enumerate(((g_hbm, gs), (q_hbm, qs))):
        for half in range(2):
            for h in range(heads):
                pltpu.make_async_copy(
                    src.at[pl.ds(half * span, span), pl.ds(h * width, width)],
                    dst.at[half, pl.ds(h * span, span), :],
                    load_sem.at[at],
                ).start()
    o_copy = pltpu.make_async_copy(o_hbm, o_vm, load_sem.at[2])
    o_copy.start()

    barrier = pltpu.get_barrier_semaphore()
    friends = [inner_at(s) for s in range(-REACH, REACH + 1) if s] + [outer_at(-1), outer_at(1)]
    for friend in friends:
        pl.semaphore_signal(barrier, inc=1, device_id=friend, device_id_type=pl.DeviceIdType.MESH)
    first = pos_ref[0] // span
    mark[...] = jnp.full(mark.shape, first, jnp.int32)
    for copy in loads:
        copy.wait()
    pl.semaphore_wait(barrier, len(friends))

    def put(src_slot, slot, target):
        return pltpu.make_async_remote_copy(
            src_ref=kv.at[src_slot],
            dst_ref=kv.at[slot],
            send_sem=put_sem.at[slot],
            recv_sem=get_sem.at[slot],
            device_id=target,
            device_id_type=pl.DeviceIdType.MESH,
        )

    core_mate = (outer, inner + 1 - 2 * core)
    side_mate = (outer, inner + 2 - 4 * side)
    put4 = put(0, 4, inner_at(4))
    put5 = put(0, FAR, outer_at(1))
    put2 = put(4 * side, 2, side_mate)
    put1 = put(2 * core, 1, core_mate)
    put3 = put(2 + 2 * core, 3, core_mate)
    put4.start()
    put5.start()

    @pl.when(side == 0)
    def _():
        put2.start()

    @pl.when(core == 0)
    def _():
        put1.start()

    mark_puts = []
    for slot in range(1, FAR + 1):
        copy = pltpu.make_async_remote_copy(
            src_ref=mark,
            dst_ref=marks.at[slot],
            send_sem=mark_send.at[slot],
            recv_sem=mark_recv.at[slot],
            device_id=outer_at(1) if slot == FAR else inner_at(slot),
            device_id_type=pl.DeviceIdType.MESH,
        )
        copy.start()
        mark_puts.append(copy)

    pltpu.make_async_copy(gs, gs, load_sem.at[0]).wait()
    o_copy.wait()
    lane = lax.broadcasted_iota(jnp.int32, (span, width), 1)
    spread = jnp.where(lane < 3 * heads, lax.rem(lane, heads), -1)

    def split(x):
        hi = x.astype(BF16).astype(F32)
        mid = (x - hi).astype(BF16).astype(F32)
        return jnp.where(lane < heads, hi, jnp.where(lane < 2 * heads, mid, x - hi - mid))

    norm_rows = jnp.concatenate(
        [lse_ref[...] * (1.0 / scale)] * 3 + [jnp.zeros((width - 3 * heads, 2 * span), F32)], 0
    )
    norm_table = norm_rows.T
    for half in range(2):
        rows = pl.ds(half * span, span)
        dots = jnp.zeros((span, width), F32)
        for h in range(heads):
            g = gs[half, pl.ds(h * span, span), :].astype(F32)
            o = o_vm[rows, pl.ds(h * width, width)].astype(F32)
            dots = jnp.where(spread == h, jnp.sum(g * o, axis=1, keepdims=True), dots)
        dots, norms = split(dots), split(norm_table[half * span : (half + 1) * span])
        for h in range(heads):
            to = pl.ds(h * span, span)
            yg[half, to, :] = jnp.where(spread == h, dots, 0.0).astype(BF16)
            yq[half, to, :] = jnp.where(spread == h, norms, 0.0).astype(BF16)
    minus = jnp.where(lane < 3 * heads, -1.0, 0.0).astype(BF16)

    columns = heads * span
    high = jnp.where(first < n_outer * n_inner, 1, 0)
    low = 1 - high

    def unit(slot, key_half, query_half, diagonal):
        k, v = (lax.select(key_half == 1, kv[slot, at, 1], kv[slot, at, 0]) for at in range(2))
        q, g = qs[query_half], gs[query_half]
        scores = nt(jnp.concatenate([k, minus], 1), jnp.concatenate([q, yq[query_half]], 1))
        probs = jnp.exp2(scores * exp_scale)
        if diagonal:
            t = lax.rem(lax.broadcasted_iota(jnp.int32, (1, columns), 1), span)
            u = lax.broadcasted_iota(jnp.int32, (span, 1), 0)
            probs = jnp.where(u <= t, probs, 0.0)
        probs_b = probs.astype(BF16)
        shifted = nt(jnp.concatenate([v, minus], 1), jnp.concatenate([g, yg[query_half]], 1))
        dscores = (probs * shifted).astype(BF16)
        return nn(dscores, q), nn(probs_b, g), tn(k, dscores)

    pltpu.make_async_copy(qs, qs, load_sem.at[1]).wait()

    dk, dv, dq = unit(0, low, low, True)
    own[0, 0], own[1, 0], dqt[0] = dk, dv, dq
    dk, dv, dq = unit(0, low, high, False)
    own[0, 0] += dk
    own[1, 0] += dv
    dqt[1] = dq
    dk, dv, dq = unit(0, high, high, True)
    own[0, 1], own[1, 1] = dk, dv
    dqt[1] += dq

    mark_loads = []
    for slot in range(1, FAR + 1):
        mark_puts[slot - 1].wait_recv()
        copy = pltpu.make_async_copy(marks.at[slot], mark_load.at[slot], mark_recv.at[slot])
        mark_loads.append(copy)
        copy.start()
    for copy in mark_loads:
        copy.wait()

    def term_put(slot):
        far = slot // FAR
        target = (
            lax.rem(outer + (n_outer - 1) * far, n_outer),
            lax.rem(inner + (n_inner - slot) * (1 - far), n_inner),
        )
        return pltpu.make_async_remote_copy(
            src_ref=terms.at[slot],
            dst_ref=came.at[slot],
            send_sem=term_send.at[slot],
            recv_sem=term_recv.at[slot],
            device_id=target,
            device_id_type=pl.DeviceIdType.MESH,
        )

    order = (4, FAR, 2, 1, 3)
    packed = sum(slot * 8**at for at, slot in enumerate(order))

    def step(_, rest):
        slot, rest = lax.rem(rest, 8), rest // 8
        put(0, slot, core_mate).wait_recv()

        @pl.when((slot == 4) & (side == 1))
        def _():
            put2.start()

        @pl.when(((slot == 4) & (core == 1)) | ((slot == 2) & (core == 0)))
        def _():
            put3.start()

        @pl.when((slot == 2) & (core == 1))
        def _():
            put1.start()

        there = mark_load[slot, 0, 0]
        there_low = jnp.where(there < n_outer * n_inner, 0, 1)
        run_here = jnp.minimum(first, 2 * n_outer * n_inner - 1 - first)
        run_there = jnp.minimum(there, 2 * n_outer * n_inner - 1 - there)
        earlier = run_there < run_here
        keep = jnp.where(earlier, 1.0, 0.0)
        dk, dv, dq = unit(slot, there_low, high, False)
        key_half = jnp.where(earlier, there_low, 1 - there_low)
        query_half = jnp.where(earlier, low, high)
        dk2, dv2, dq2 = unit(slot, key_half, query_half, False)
        dq_low = dq2 * keep
        dqt[0] += dq_low
        dqt[1] += dq + (dq2 - dq_low)
        for at, (one, two) in enumerate(((dk, dk2), (dv, dv2))):
            two_low = two * keep
            factor = 1.0 if at else scale
            terms[slot, at, 0] = ((one + two_low) * factor).astype(BF16)
            terms[slot, at, 1] = ((two - two_low) * factor).astype(BF16)
        term_put(slot).start()
        return rest

    lax.fori_loop(0, len(order), step, packed)

    for half in range(2):
        rank = jnp.where(first < n_outer * n_inner, half, 1 - half)
        dq = (dqt[rank] * scale).T.astype(BF16)
        for h in range(heads):
            dq_ref[pl.ds(half * span, span), pl.ds(h * width, width)] = dq[h * span : (h + 1) * span]

    for slot in range(1, FAR + 1):
        term_put(jnp.int32(slot)).wait_recv()
    for at, out in enumerate((dk_ref, dv_ref)):
        for half in range(2):
            rank = jnp.where(first < n_outer * n_inner, half, 1 - half)
            total = own[at, rank] * (1.0 if at else scale)
            for slot in range(1, FAR + 1):
                total += came[slot, at, rank].astype(F32)
            out[pl.ds(half * span, span), :] = total.astype(BF16)

    for copy in mark_puts:
        copy.wait_send()
    for copy in (put1, put2, put3, put4, put5):
        copy.wait_send()
    for slot in range(1, FAR + 1):
        term_put(jnp.int32(slot)).wait_send()


def shards(queries, keys, values, saved_out, saved_lse, out_grad, positions):
    rows, columns = queries.shape
    width = keys.shape[1]
    span = rows // 2
    heads = columns // width
    anywhere = pl.BlockSpec(memory_space=pl.ANY)
    vmem = pl.BlockSpec(memory_space=pltpu.VMEM)
    slots = FAR + 1
    stack = (2, heads * span, width)
    pair = (2, 2, span, width)
    dma = pltpu.SemaphoreType.DMA
    return pl.pallas_call(
        functools.partial(kernel, lax.axis_size("outer"), lax.axis_size("inner")),
        out_shape=(
            jax.ShapeDtypeStruct(queries.shape, BF16),
            jax.ShapeDtypeStruct(keys.shape, BF16),
            jax.ShapeDtypeStruct(values.shape, BF16),
        ),
        in_specs=[
            anywhere,
            anywhere,
            anywhere,
            anywhere,
            vmem,
            anywhere,
            pl.BlockSpec(memory_space=pltpu.SMEM),
        ],
        out_specs=[vmem] * 3,
        scratch_shapes=[
            pltpu.VMEM(stack, BF16),
            pltpu.VMEM(stack, BF16),
            pltpu.VMEM(stack, BF16),
            pltpu.VMEM(stack, BF16),
            pltpu.VMEM((rows, columns), BF16),
            pltpu.VMEM((slots,) + pair, BF16),
            pltpu.VMEM((8, 128), jnp.int32),
            pltpu.VMEM((slots, 8, 128), jnp.int32),
            pltpu.VMEM((2, width, heads * span), F32),
            pltpu.VMEM(pair, F32),
            pltpu.VMEM((slots,) + pair, BF16),
            pltpu.VMEM((slots,) + pair, BF16),
            dma((3,)),
            dma((2, 2)),
            dma((slots,)),
            dma((slots,)),
            pltpu.SMEM((slots, 8, 128), jnp.int32),
            dma((slots,)),
            dma((slots,)),
            dma((slots,)),
            dma((slots,)),
        ],
        compiler_params=pltpu.CompilerParams(
            collective_id=0, has_side_effects=True, vmem_limit_bytes=56 * 2**20
        ),
    )(queries, keys, values, saved_out, saved_lse.T, out_grad, positions)


def solution(mesh):
    rows = P(("outer", "inner"), None)
    return jax.shard_map(
        shards,
        mesh=mesh,
        in_specs=(rows,) * 6 + (P(("outer", "inner")),),
        out_specs=(rows,) * 3,
        check_vma=False,
    )
```

profile of v0, /device:TPU:1, one launch (start us, length us, event | category | flops | bytes accessed | tf_op | source)
XLA Modules:
  0.0 46.7 jit_solution(11894474554171413011)
XLA Ops:
  0.6 42.4 %shard_map.94 = (bf16[384,1024]{1,0:T(8,128)(2,1)}, bf16[384,128]{1,0:T(8,128)(2,1)}, bf16[384,128]{1,0:T(8,128)(2,1)}) custom-call(bf16[384,1024]{1,0:T(8,128)(2,1)} %q_hbm.1, bf16[384,128]{1,0:T(8,128)(2,1)} %k_hbm.1, bf16[384,128]{1,0:T(8,128)(2,1)} %v_hbm.1, bf16[384,1024]{1,0:T(8,128)(2,1)} %o_hbm.1, f32[8,384]{1,0:T(8,128)} %bitcast.1, ...), custom_call_target="tpu_custom_call" | custom-call | tf_op jit(solution)/shard_map/pallas_call | solution.py:309
  43.0 0.0 copy-start.1
  43.0 2.1 %copy.13 = bf16[384,1024]{1,0:T(8,128)(2,1)} copy(bf16[384,1024]{1,0:T(8,128)(2,1)} %get-tuple-element.6) | data formatting | bytes 1572864
  45.1 0.0 copy-done.1
  45.1 0.0 copy-start
  45.1 0.6 %copy.14 = bf16[384,128]{1,0:T(8,128)(2,1)} copy(bf16[384,128]{1,0:T(8,128)(2,1)S(1)} %copy-done.1) | data formatting | bytes 196608
  45.8 0.3 copy-done
  46.1 0.6 %copy.15 = bf16[384,128]{1,0:T(8,128)(2,1)} copy(bf16[384,128]{1,0:T(8,128)(2,1)S(1)} %copy-done) | data formatting | bytes 196608
Async XLA Ops:
  43.0 2.1 %copy-start.1 = (bf16[384,128]{1,0:T(8,128)(2,1)S(1)}, bf16[384,128]{1,0:T(8,128)(2,1)}, u32[]{:S(2)}) copy-start(bf16[384,128]{1,0:T(8,128)(2,1)} %get-tuple-element.7) | copy-start | bytes 294916
  45.1 0.9 %copy-start = (bf16[384,128]{1,0:T(8,128)(2,1)S(1)}, bf16[384,128]{1,0:T(8,128)(2,1)}, u32[]{:S(2)}) copy-start(bf16[384,128]{1,0:T(8,128)(2,1)} %get-tuple-element.8) | copy-start | bytes 294916
where the time goes:
time: 46.9 us; the launch traced here: 46.7 us
  Pallas kernels  42.4 us (90%)
  local copies, waits for them, and re-layouts  3.67 us (8%)
  between operations  0.65 us (1%)
    pallas_call x1, Pallas kernels, shards(): pl.pallas_call(functools.partial(kernel, lax.axis_size('outer'), lax.axis...  42.4 us
    unnamed x7, local copies, waits for them, and re-layouts  3.67 us

commit v1 on v0

--- a/solution.py
+++ b/solution.py
@@ -60,6 +60,7 @@
     get_sem,
     term_send,
     term_recv,
+    gate,
 ):
     outer = lax.axis_index("outer")
     inner = lax.axis_index("inner")
@@ -68,7 +69,6 @@
     scale = width**-0.5
     exp_scale = float(np.log2(np.e)) * scale
     core = lax.rem(inner, 2)
-    side = lax.rem(inner // 2, 2)
 
     def inner_at(step):
         return (outer, lax.rem(inner + n_inner + step, n_inner))
@@ -84,7 +84,37 @@
             )
             copy.start()
             loads.append(copy)
-    tiles = []
+
+    def remote(src, dst, send_sem, recv_sem, target):
+        return pltpu.make_async_remote_copy(
+            src_ref=src,
+            dst_ref=dst,
+            send_sem=send_sem,
+            recv_sem=recv_sem,
+            device_id=target,
+            device_id_type=pl.DeviceIdType.MESH,
+        )
+
+    def signal(semaphore, target):
+        pl.semaphore_signal(semaphore, 1, device_id=target, device_id_type=pl.DeviceIdType.MESH)
+
+    barrier = pltpu.get_barrier_semaphore()
+    mate = (outer, inner + 1 - 2 * core)
+
+    @pl.when(core == 0)
+    def _():
+        for step in (-4, -2, 2, 4):
+            signal(barrier, inner_at(step))
+        for step in (-1, 1):
+            signal(barrier, (outer_at(step)[0], inner + 1))
+
+    @pl.when(core == 1)
+    def _():
+        for step in (-5, -3, -1, 1, 3):
+            signal(barrier, inner_at(step))
+        for step in (-1, 1):
+            signal(barrier, outer_at(step))
+
     for at, (src, dst) in enumerate(((g_hbm, gs), (q_hbm, qs))):
         for half in range(2):
             for h in range(heads):
@@ -93,59 +123,69 @@
                     dst.at[half, pl.ds(h * span, span), :],
                     load_sem.at[at],
                 ).start()
-    o_copy = pltpu.make_async_copy(o_hbm, o_vm, load_sem.at[2])
-    o_copy.start()
-
-    barrier = pltpu.get_barrier_semaphore()
-    friends = [inner_at(s) for s in range(-REACH, REACH + 1) if s] + [outer_at(-1), outer_at(1)]
-    for friend in friends:
-        pl.semaphore_signal(barrier, inc=1, device_id=friend, device_id_type=pl.DeviceIdType.MESH)
+        if at == 0:
+            o_copy = pltpu.make_async_copy(o_hbm, o_vm, load_sem.at[2])
+            o_copy.start()
     first = pos_ref[0] // span
     mark[...] = jnp.full(mark.shape, first, jnp.int32)
     for copy in loads:
         copy.wait()
-    pl.semaphore_wait(barrier, len(friends))
+
+    @pl.when(core == 0)
+    def _():
+        pl.semaphore_wait(barrier, 9)
+        signal(gate, mate)
+
+    @pl.when(core == 1)
+    def _():
+        pl.semaphore_wait(gate, 1)
 
     def put(src_slot, slot, target):
-        return pltpu.make_async_remote_copy(
-            src_ref=kv.at[src_slot],
-            dst_ref=kv.at[slot],
-            send_sem=put_sem.at[slot],
-            recv_sem=get_sem.at[slot],
-            device_id=target,
-            device_id_type=pl.DeviceIdType.MESH,
+        return remote(kv.at[src_slot], kv.at[slot], put_sem.at[slot], get_sem.at[slot], target)
+
+    put5 = put(0, FAR, outer_at(1))
+    put4 = put(0, 4, inner_at(4))
+    put2 = put(0, 2, inner_at(2))
+    put1 = put(2 * core, 1, mate)
+    put3 = put(2 + 2 * core, 3, mate)
+    mark_puts = [
+        remote(
+            mark,
+            marks.at[slot],
+            mark_send.at[slot],
+            mark_recv.at[slot],
+            outer_at(1) if slot == FAR else inner_at(slot),
         )
-
-    core_mate = (outer, inner + 1 - 2 * core)
-    side_mate = (outer, inner + 2 - 4 * side)
-    put4 = put(0, 4, inner_at(4))
-    put5 = put(0, FAR, outer_at(1))
-    put2 = put(4 * side, 2, side_mate)
-    put1 = put(2 * core, 1, core_mate)
-    put3 = put(2 + 2 * core, 3, core_mate)
+        for slot in range(1, FAR + 1)
+    ]
+    for copy in mark_puts[:REACH]:
+        copy.start()
+
+    @pl.when(core == 0)
+    def _():
+        put1.start()
+
     put4.start()
-    put5.start()
-
-    @pl.when(side == 0)
-    def _():
-        put2.start()
-
-    @pl.when(core == 0)
-    def _():
-        put1.start()
-
-    mark_puts = []
-    for slot in range(1, FAR + 1):
-        copy = pltpu.make_async_remote_copy(
-            src_ref=mark,
-            dst_ref=marks.at[slot],
-            send_sem=mark_send.at[slot],
-            recv_sem=mark_recv.at[slot],
-            device_id=outer_at(1) if slot == FAR else inner_at(slot),
-            device_id_type=pl.DeviceIdType.MESH,
-        )
-        copy.start()
-        mark_puts.append(copy)
+    put2.start()
+
+    def reach_outer():
+        @pl.when(core == 1)
+        def _():
+            pl.semaphore_wait(barrier, 4)
+            signal(gate, mate)
+
+        @pl.when(core == 0)
+        def _():
+            pl.semaphore_wait(gate, 1)
+
+        mark_puts[REACH].start()
+        put5.start()
+
+    early = lax.rem(outer, 8) == 0
+
+    @pl.when(jnp.logical_not(early))
+    def _():
+        reach_outer()
 
     pltpu.make_async_copy(gs, gs, load_sem.at[0]).wait()
     o_copy.wait()
@@ -205,48 +245,66 @@
     own[0, 1], own[1, 1] = dk, dv
     dqt[1] += dq
 
-    mark_loads = []
-    for slot in range(1, FAR + 1):
+    def mark_in(slot):
         mark_puts[slot - 1].wait_recv()
-        copy = pltpu.make_async_copy(marks.at[slot], mark_load.at[slot], mark_recv.at[slot])
-        mark_loads.append(copy)
+        return pltpu.make_async_copy(marks.at[slot], mark_load.at[slot], mark_recv.at[slot])
+
+    mark_loads = [mark_in(slot) for slot in range(1, REACH + 1)]
+    for copy in mark_loads:
         copy.start()
+
+    @pl.when(early)
+    def _():
+        reach_outer()
+
     for copy in mark_loads:
         copy.wait()
 
-    def term_put(slot):
-        far = slot // FAR
-        target = (
-            lax.rem(outer + (n_outer - 1) * far, n_outer),
-            lax.rem(inner + (n_inner - slot) * (1 - far), n_inner),
-        )
-        return pltpu.make_async_remote_copy(
-            src_ref=terms.at[slot],
-            dst_ref=came.at[slot],
-            send_sem=term_send.at[slot],
-            recv_sem=term_recv.at[slot],
-            device_id=target,
-            device_id_type=pl.DeviceIdType.MESH,
-        )
-
-    order = (4, FAR, 2, 1, 3)
-    packed = sum(slot * 8**at for at, slot in enumerate(order))
-
-    def step(_, rest):
+    targets = {1: mate, 2: inner_at(-2), 3: mate, 4: inner_at(-4), FAR: outer_at(-1)}
+    term_put = {
+        slot: remote(terms.at[slot], came.at[slot], term_send.at[slot], term_recv.at[slot], targets[slot])
+        for slot in targets
+    }
+
+    def merge(slot, other):
+        for at in range(2):
+            for half in range(2):
+                both = terms[slot, at, half].astype(F32) + came[other, at, half].astype(F32)
+                terms[slot, at, half] = both.astype(BF16)
+
+    soon = 1 - jnp.minimum(lax.rem(outer, 8), 1)
+
+    def step(at_step, rest):
         slot, rest = lax.rem(rest, 8), rest // 8
-        put(0, slot, core_mate).wait_recv()
-
-        @pl.when((slot == 4) & (side == 1))
-        def _():
-            put2.start()
-
-        @pl.when(((slot == 4) & (core == 1)) | ((slot == 2) & (core == 0)))
-        def _():
+
+        @pl.when(slot == FAR)
+        def _():
+            copy = mark_in(FAR)
+            copy.start()
+            copy.wait()
+
+        @pl.when((at_step == 1) & (core == 1))
+        def _():
+            put4.wait_recv()
             put3.start()
 
-        @pl.when((slot == 2) & (core == 1))
-        def _():
+        @pl.when((at_step == 2) & (core == 0))
+        def _():
+            put2.wait_recv()
+            put3.start()
+
+        @pl.when((at_step == 3 - soon) & (core == 1))
+        def _():
+            put2.wait_recv()
             put1.start()
+
+        @pl.when((slot != 2) & (slot + core != 5))
+        def _():
+            put(0, slot, mate).wait_recv()
+
+        @pl.when((slot == FAR) & (core == 0))
+        def _():
+            put5.wait_recv()
 
         there = mark_load[slot, 0, 0]
         there_low = jnp.where(there < n_outer * n_inner, 0, 1)
@@ -266,33 +324,95 @@
             factor = 1.0 if at else scale
             terms[slot, at, 0] = ((one + two_low) * factor).astype(BF16)
             terms[slot, at, 1] = ((two - two_low) * factor).astype(BF16)
-        term_put(slot).start()
+
+        @pl.when(slot == FAR)
+        def _():
+            term_put[FAR].start()
+
+        @pl.when(slot == 1)
+        def _():
+            term_put[1].start()
+
+        @pl.when(slot == 3)
+        def _():
+            term_put[3].start()
+
+        @pl.when((slot == 4) & (core == 0))
+        def _():
+            term_put[4].start()
+
+        @pl.when((slot == 3) & (core == 1))
+        def _():
+            term_put[3].wait_recv()
+            merge(4, 3)
+            term_put[4].start()
+
+        @pl.when((slot == 2) & (core == 0))
+        def _():
+            term_put[3].wait_recv()
+            merge(2, 3)
+            term_put[2].start()
+
+        @pl.when((slot == 2) & (core == 1))
+        def _():
+            term_put[1].wait_recv()
+            merge(2, 1)
+            term_put[2].start()
+
         return rest
 
-    lax.fori_loop(0, len(order), step, packed)
-
+    def packed(*order):
+        return sum(slot * 8**at for at, slot in enumerate(order))
+
+    orders = (
+        (packed(FAR, 3, 4, 1, 2), packed(4, 3, 1, 2, FAR)),
+        (packed(1, FAR, 4, 3, 2), packed(1, 4, 3, 2, FAR)),
+    )
+    even, odd = (late * (1 - soon) + ahead * soon for late, ahead in orders)
+    lax.fori_loop(0, FAR, step, even * (1 - core) + odd * core)
+
+    in_order = first < n_outer * n_inner
+    dq_out = []
     for half in range(2):
-        rank = jnp.where(first < n_outer * n_inner, half, 1 - half)
+        rank = jnp.where(in_order, half, 1 - half)
+        rows = pl.ds(half * span, span)
         dq = (dqt[rank] * scale).T.astype(BF16)
         for h in range(heads):
-            dq_ref[pl.ds(half * span, span), pl.ds(h * width, width)] = dq[h * span : (h + 1) * span]
-
-    for slot in range(1, FAR + 1):
-        term_put(jnp.int32(slot)).wait_recv()
+            o_vm[rows, pl.ds(h * width, width)] = dq[h * span : (h + 1) * span]
+        copy = pltpu.make_async_copy(o_vm.at[rows, :], dq_ref.at[rows, :], kv_sem.at[0, half])
+        copy.start()
+        dq_out.append(copy)
+
+    @pl.when(core == 0)
+    def _():
+        term_put[1].wait_recv()
+
+    for slot in (2, 4, FAR):
+        term_put[slot].wait_recv()
+    from_mate = jnp.where(core == 0, 1.0, 0.0)
     for at, out in enumerate((dk_ref, dv_ref)):
         for half in range(2):
-            rank = jnp.where(first < n_outer * n_inner, half, 1 - half)
-            total = own[at, rank] * (1.0 if at else scale)
-            for slot in range(1, FAR + 1):
+            rank = jnp.where(in_order, half, 1 - half)
+            total = own[at, rank] * (1.0 if at else scale) + came[1, at, rank].astype(F32) * from_mate
+            for slot in (2, 4, FAR):
                 total += came[slot, at, rank].astype(F32)
             out[pl.ds(half * span, span), :] = total.astype(BF16)
 
-    for copy in mark_puts:
+    for copy in mark_puts + [put1, put2, put3, put4, put5] + list(term_put.values()):
         copy.wait_send()
-    for copy in (put1, put2, put3, put4, put5):
-        copy.wait_send()
-    for slot in range(1, FAR + 1):
-        term_put(jnp.int32(slot)).wait_send()
+    for copy in dq_out:
+        copy.wait()
+
+
+def hand_over(*refs):
+    count = len(refs) // 2
+    copies = [
+        pltpu.make_async_copy(refs[at], refs[count + at], refs[-1].at[at]) for at in range(count)
+    ]
+    for copy in copies:
+        copy.start()
+    for copy in copies:
+        copy.wait()
 
 
 def shards(queries, keys, values, saved_out, saved_lse, out_grad, positions):
@@ -306,7 +426,7 @@
     stack = (2, heads * span, width)
     pair = (2, 2, span, width)
     dma = pltpu.SemaphoreType.DMA
-    return pl.pallas_call(
+    results = pl.pallas_call(
         functools.partial(kernel, lax.axis_size("outer"), lax.axis_size("inner")),
         out_shape=(
             jax.ShapeDtypeStruct(queries.shape, BF16),
@@ -322,7 +442,7 @@
             anywhere,
             pl.BlockSpec(memory_space=pltpu.SMEM),
         ],
-        out_specs=[vmem] * 3,
+        out_specs=[anywhere, vmem, vmem],
         scratch_shapes=[
             pltpu.VMEM(stack, BF16),
             pltpu.VMEM(stack, BF16),
@@ -345,11 +465,19 @@
             dma((slots,)),
             dma((slots,)),
             dma((slots,)),
+            pltpu.SemaphoreType.REGULAR,
         ],
         compiler_params=pltpu.CompilerParams(
             collective_id=0, has_side_effects=True, vmem_limit_bytes=56 * 2**20
         ),
     )(queries, keys, values, saved_out, saved_lse.T, out_grad, positions)
+    return pl.pallas_call(
+        hand_over,
+        out_shape=tuple(jax.ShapeDtypeStruct(x.shape, x.dtype) for x in results),
+        in_specs=[anywhere] * 3,
+        out_specs=[anywhere] * 3,
+        scratch_shapes=[dma((3,))],
+    )(*results)
 
 
 def solution(mesh):

time: 46.9 us -> 68.9 us (1.47)
  the two profiles are of different devices: /device:TPU:1 before, /device:TPU:224 now
where the time goes in v1:
time: 68.9 us; the launch traced here: 67.7 us
  Pallas kernels  67.1 us (97%)
    pallas_call x1, Pallas kernels, shards(): pl.pallas_call(functools.partial(kernel, lax.axis_size('outer'), lax.axis...  36.1 us
    pallas_call x1, Pallas kernels, shards(): pl.pallas_call(hand_over, out_shape=tuple((jax.ShapeDtypeStruct(x.shape,...  30.9 us

profile of v1, /device:TPU:224, one launch (start us, length us, event | category | flops | bytes accessed | tf_op | source)
XLA Modules:
  0.0 67.7 jit_solution(12082063859531619982)
XLA Ops:
  0.6 36.1 %shard_map.94 = (bf16[384,1024]{1,0:T(8,128)(2,1)}, bf16[384,128]{1,0:T(8,128)(2,1)}, bf16[384,128]{1,0:T(8,128)(2,1)}) custom-call(bf16[384,1024]{1,0:T(8,128)(2,1)} %q_hbm.1, bf16[384,128]{1,0:T(8,128)(2,1)} %k_hbm.1, bf16[384,128]{1,0:T(8,128)(2,1)} %v_hbm.1, bf16[384,1024]{1,0:T(8,128)(2,1)} %o_hbm.1, f32[8,384]{1,0:T(8,128)} %bitcast.1, ...), custom_call_target="tpu_custom_call" | custom-call | tf_op jit(solution)/shard_map/pallas_call | solution.py:429
  36.8 30.9 %shard_map.95 = (bf16[384,1024]{1,0:T(8,128)(2,1)}, bf16[384,128]{1,0:T(8,128)(2,1)}, bf16[384,128]{1,0:T(8,128)(2,1)}) custom-call(bf16[384,1024]{1,0:T(8,128)(2,1)} %get-tuple-element.6.refs_0_, bf16[384,128]{1,0:T(8,128)(2,1)} %get-tuple-element.7.refs_1_, bf16[384,128]{1,0:T(8,128)(2,1)} %get-tuple-element.8.refs_2_), custom_call_target="tpu_custom_call" | custom-call | tf_op jit(solution)/shard_map/pallas_call | solution.py:474

commit v2 on v1

--- a/solution.py
+++ b/solution.py
@@ -69,6 +69,7 @@
     scale = width**-0.5
     exp_scale = float(np.log2(np.e)) * scale
     core = lax.rem(inner, 2)
+    side = lax.rem(inner // 2, 2)
 
     def inner_at(step):
         return (outer, lax.rem(inner + n_inner + step, n_inner))
@@ -164,9 +165,11 @@
     @pl.when(core == 0)
     def _():
         put1.start()
-
-    put4.start()
-    put2.start()
+        put4.start()
+
+    @pl.when(side == 0)
+    def _():
+        put2.start()
 
     def reach_outer():
         @pl.when(core == 1)
@@ -213,6 +216,11 @@
             to = pl.ds(h * span, span)
             yg[half, to, :] = jnp.where(spread == h, dots, 0.0).astype(BF16)
             yq[half, to, :] = jnp.where(spread == h, norms, 0.0).astype(BF16)
+
+    @pl.when(core == 1)
+    def _():
+        put4.start()
+
     minus = jnp.where(lane < 3 * heads, -1.0, 0.0).astype(BF16)
 
     columns = heads * span
@@ -253,6 +261,10 @@
     for copy in mark_loads:
         copy.start()
 
+    @pl.when(side == 1)
+    def _():
+        put2.start()
+
     @pl.when(early)
     def _():
         reach_outer()
@@ -260,7 +272,7 @@
     for copy in mark_loads:
         copy.wait()
 
-    targets = {1: mate, 2: inner_at(-2), 3: mate, 4: inner_at(-4), FAR: outer_at(-1)}
+    targets = {1: mate, 2: inner_at(-2), 3: inner_at(2 * core - 3), 4: inner_at(-4), FAR: outer_at(-1)}
     term_put = {
         slot: remote(terms.at[slot], came.at[slot], term_send.at[slot], term_recv.at[slot], targets[slot])
         for slot in targets
@@ -288,23 +300,21 @@
             put4.wait_recv()
             put3.start()
 
-        @pl.when((at_step == 2) & (core == 0))
+        @pl.when(at_step == 3 - soon)
         def _():
             put2.wait_recv()
+
+        @pl.when((at_step == 3 - soon) & (core == 0))
+        def _():
             put3.start()
 
         @pl.when((at_step == 3 - soon) & (core == 1))
         def _():
-            put2.wait_recv()
             put1.start()
 
-        @pl.when((slot != 2) & (slot + core != 5))
+        @pl.when(jnp.logical_not((slot == 2) | ((slot == 4) & (core == 1))))
         def _():
             put(0, slot, mate).wait_recv()
-
-        @pl.when((slot == FAR) & (core == 0))
-        def _():
-            put5.wait_recv()
 
         there = mark_load[slot, 0, 0]
         there_low = jnp.where(there < n_outer * n_inner, 0, 1)
@@ -325,27 +335,11 @@
             terms[slot, at, 0] = ((one + two_low) * factor).astype(BF16)
             terms[slot, at, 1] = ((two - two_low) * factor).astype(BF16)
 
-        @pl.when(slot == FAR)
-        def _():
-            term_put[FAR].start()
-
-        @pl.when(slot == 1)
-        def _():
-            term_put[1].start()
-
-        @pl.when(slot == 3)
-        def _():
-            term_put[3].start()
-
-        @pl.when((slot == 4) & (core == 0))
-        def _():
-            term_put[4].start()
-
-        @pl.when((slot == 3) & (core == 1))
-        def _():
-            term_put[3].wait_recv()
-            merge(4, 3)
-            term_put[4].start()
+        for sent in (1, 3, 4, FAR):
+
+            @pl.when(slot == sent)
+            def _():
+                term_put[sent].start()
 
         @pl.when((slot == 2) & (core == 0))
         def _():
@@ -353,7 +347,7 @@
             merge(2, 3)
             term_put[2].start()
 
-        @pl.when((slot == 2) & (core == 1))
+        @pl.when((slot == 3) & (core == 1))
         def _():
             term_put[1].wait_recv()
             merge(2, 1)
@@ -365,8 +359,8 @@
         return sum(slot * 8**at for at, slot in enumerate(order))
 
     orders = (
-        (packed(FAR, 3, 4, 1, 2), packed(4, 3, 1, 2, FAR)),
-        (packed(1, FAR, 4, 3, 2), packed(1, 4, 3, 2, FAR)),
+        (packed(4, FAR, 3, 1, 2), packed(4, 3, 1, 2, FAR)),
+        (packed(1, 4, FAR, 2, 3), packed(1, 4, 2, 3, FAR)),
     )
     even, odd = (late * (1 - soon) + ahead * soon for late, ahead in orders)
     lax.fori_loop(0, FAR, step, even * (1 - core) + odd * core)
@@ -387,14 +381,17 @@
     def _():
         term_put[1].wait_recv()
 
+    @pl.when(core == 1)
+    def _():
+        term_put[3].wait_recv()
+
     for slot in (2, 4, FAR):
         term_put[slot].wait_recv()
-    from_mate = jnp.where(core == 0, 1.0, 0.0)
     for at, out in enumerate((dk_ref, dv_ref)):
         for half in range(2):
             rank = jnp.where(in_order, half, 1 - half)
-            total = own[at, rank] * (1.0 if at else scale) + came[1, at, rank].astype(F32) * from_mate
-            for slot in (2, 4, FAR):
+            total = own[at, rank] * (1.0 if at else scale)
+            for slot in (1 + 2 * core, 2, 4, FAR):
                 total += came[slot, at, rank].astype(F32)
             out[pl.ds(half * span, span), :] = total.astype(BF16)
 
@@ -404,14 +401,19 @@
         copy.wait()
 
 
-def hand_over(*refs):
-    count = len(refs) // 2
-    copies = [
-        pltpu.make_async_copy(refs[at], refs[count + at], refs[-1].at[at]) for at in range(count)
-    ]
-    for copy in copies:
+def hand_over(dq, dk, dv, dq_out, dk_out, dv_out, dq_vm, dk_vm, dv_vm, sem):
+    rows = dq.shape[0] // 4
+    parts = [pl.ds(at * rows, rows) for at in range(4)]
+    routes = [(dq.at[part, :], dq_vm.at[part, :], dq_out.at[part, :]) for part in parts]
+    routes += [(dk, dk_vm, dk_out), (dv, dv_vm, dv_out)]
+    ins = [pltpu.make_async_copy(a, b, sem.at[0, at]) for at, (a, b, _) in enumerate(routes)]
+    outs = [pltpu.make_async_copy(b, c, sem.at[1, at]) for at, (_, b, c) in enumerate(routes)]
+    for copy in ins:
         copy.start()
-    for copy in copies:
+    for came, goes in zip(ins, outs):
+        came.wait()
+        goes.start()
+    for copy in outs:
         copy.wait()
 
 
@@ -476,7 +478,7 @@
         out_shape=tuple(jax.ShapeDtypeStruct(x.shape, x.dtype) for x in results),
         in_specs=[anywhere] * 3,
         out_specs=[anywhere] * 3,
-        scratch_shapes=[dma((3,))],
+        scratch_shapes=[pltpu.VMEM(x.shape, x.dtype) for x in results] + [dma((2, 6))],
     )(*results)
 
 

time: 68.9 us -> 38 us (0.55); the launches traced: 67.7 us -> 37.8 us
  Pallas kernels: 67.1 us -> 37.2 us
    pallas_call x1, Pallas kernels: 30.9 us -> 2.06 us  [shards(): pl.pallas_call(hand_over, out_shape=tuple((jax.ShapeDtypeStruct(x.shape,...]
    pallas_call x1, Pallas kernels: 36.1 us -> 35.1 us  [shards(): pl.pallas_call(functools.partial(kernel, lax.axis_size('outer'), lax.axis...]
where the time goes in v2:
time: 38 us; the launch traced here: 37.8 us
  Pallas kernels  37.2 us (98%)
  between operations  0.64 us (2%)
    pallas_call x1, Pallas kernels, shards(): pl.pallas_call(functools.partial(kernel, lax.axis_size('outer'), lax.axis...  35.1 us
    pallas_call x1, Pallas kernels, shards(): pl.pallas_call(hand_over, out_shape=tuple((jax.ShapeDtypeStruct(x.shape,...  2.06 us

profile of v2, /device:TPU:224, one launch (start us, length us, event | category | flops | bytes accessed | tf_op | source)
XLA Modules:
  0.0 37.8 jit_solution(1591180583299488115)
XLA Ops:
  0.6 35.1 %shard_map.94 = (bf16[384,1024]{1,0:T(8,128)(2,1)}, bf16[384,128]{1,0:T(8,128)(2,1)}, bf16[384,128]{1,0:T(8,128)(2,1)}) custom-call(bf16[384,1024]{1,0:T(8,128)(2,1)} %q_hbm.1, bf16[384,128]{1,0:T(8,128)(2,1)} %k_hbm.1, bf16[384,128]{1,0:T(8,128)(2,1)} %v_hbm.1, bf16[384,1024]{1,0:T(8,128)(2,1)} %o_hbm.1, f32[8,384]{1,0:T(8,128)} %bitcast.1, ...), custom_call_target="tpu_custom_call" | custom-call | tf_op jit(solution)/shard_map/pallas_call | solution.py:431
  35.7 2.1 %shard_map.95 = (bf16[384,1024]{1,0:T(8,128)(2,1)}, bf16[384,128]{1,0:T(8,128)(2,1)}, bf16[384,128]{1,0:T(8,128)(2,1)}) custom-call(bf16[384,1024]{1,0:T(8,128)(2,1)} %get-tuple-element.6.dq, bf16[384,128]{1,0:T(8,128)(2,1)} %get-tuple-element.7.dk, bf16[384,128]{1,0:T(8,128)(2,1)} %get-tuple-element.8.dv), custom_call_target="tpu_custom_call" | custom-call | tf_op jit(solution)/shard_map/pallas_call | solution.py:476

commit v3 on v2

--- a/solution.py
+++ b/solution.py
@@ -33,9 +33,9 @@
     k_hbm,
     v_hbm,
     o_hbm,
-    lse_ref,
+    lse_hbm,
     g_hbm,
-    pos_ref,
+    pos_hbm,
     dq_ref,
     dk_ref,
     dv_ref,
@@ -61,6 +61,9 @@
     term_send,
     term_recv,
     gate,
+    lse_ref,
+    pos_ref,
+    small_sem,
 ):
     outer = lax.axis_index("outer")
     inner = lax.axis_index("inner")
@@ -77,15 +80,6 @@
     def outer_at(step):
         return (lax.rem(outer + n_outer + step, n_outer), inner)
 
-    loads = []
-    for src, dst in ((k_hbm, 0), (v_hbm, 1)):
-        for half in range(2):
-            copy = pltpu.make_async_copy(
-                src.at[pl.ds(half * span, span), :], kv.at[0, dst, half], kv_sem.at[dst, half]
-            )
-            copy.start()
-            loads.append(copy)
-
     def remote(src, dst, send_sem, recv_sem, target):
         return pltpu.make_async_remote_copy(
             src_ref=src,
@@ -115,6 +109,19 @@
             signal(barrier, inner_at(step))
         for step in (-1, 1):
             signal(barrier, outer_at(step))
+
+    loads = []
+    for at, (src, dst) in enumerate(((pos_hbm, pos_ref), (lse_hbm, lse_ref))):
+        copy = pltpu.make_async_copy(src, dst, small_sem.at[at])
+        copy.start()
+        loads.append(copy)
+    for src, dst in ((k_hbm, 0), (v_hbm, 1)):
+        for half in range(2):
+            copy = pltpu.make_async_copy(
+                src.at[pl.ds(half * span, span), :], kv.at[0, dst, half], kv_sem.at[dst, half]
+            )
+            copy.start()
+            loads.append(copy)
 
     for at, (src, dst) in enumerate(((g_hbm, gs), (q_hbm, qs))):
         for half in range(2):
@@ -127,10 +134,10 @@
         if at == 0:
             o_copy = pltpu.make_async_copy(o_hbm, o_vm, load_sem.at[2])
             o_copy.start()
+    for copy in loads:
+        copy.wait()
     first = pos_ref[0] // span
     mark[...] = jnp.full(mark.shape, first, jnp.int32)
-    for copy in loads:
-        copy.wait()
 
     @pl.when(core == 0)
     def _():
@@ -165,11 +172,16 @@
     @pl.when(core == 0)
     def _():
         put1.start()
+
+    @pl.when((side == 0) & (core == 0))
+    def _():
         put4.start()
 
-    @pl.when(side == 0)
+    @pl.when((side == 0) | (core == 0))
     def _():
         put2.start()
+
+    early = lax.rem(outer, 8) == 0
 
     def reach_outer():
         @pl.when(core == 1)
@@ -182,9 +194,10 @@
             pl.semaphore_wait(gate, 1)
 
         mark_puts[REACH].start()
-        put5.start()
-
-    early = lax.rem(outer, 8) == 0
+
+        @pl.when(early | (core == 0))
+        def _():
+            put5.start()
 
     @pl.when(jnp.logical_not(early))
     def _():
@@ -217,10 +230,6 @@
             yg[half, to, :] = jnp.where(spread == h, dots, 0.0).astype(BF16)
             yq[half, to, :] = jnp.where(spread == h, norms, 0.0).astype(BF16)
 
-    @pl.when(core == 1)
-    def _():
-        put4.start()
-
     minus = jnp.where(lane < 3 * heads, -1.0, 0.0).astype(BF16)
 
     columns = heads * span
@@ -245,6 +254,19 @@
 
     dk, dv, dq = unit(0, low, low, True)
     own[0, 0], own[1, 0], dqt[0] = dk, dv, dq
+
+    @pl.when((side == 0) & (core == 1))
+    def _():
+        put4.start()
+
+    @pl.when((side == 1) & (core == 1))
+    def _():
+        put2.start()
+
+    @pl.when(jnp.logical_not(early) & (core == 1))
+    def _():
+        put5.start()
+
     dk, dv, dq = unit(0, low, high, False)
     own[0, 0] += dk
     own[1, 0] += dv
@@ -263,7 +285,7 @@
 
     @pl.when(side == 1)
     def _():
-        put2.start()
+        put4.start()
 
     @pl.when(early)
     def _():
@@ -284,7 +306,28 @@
                 both = terms[slot, at, half].astype(F32) + came[other, at, half].astype(F32)
                 terms[slot, at, half] = both.astype(BF16)
 
-    soon = 1 - jnp.minimum(lax.rem(outer, 8), 1)
+    def packed(*order):
+        return sum(slot * 8**at for at, slot in enumerate(order))
+
+    plans = (
+        (packed(4, 1, 2, FAR, 3), 0, 9, 2),
+        (packed(1, 4, 3, 2, FAR), 1, 1, 3),
+        (packed(2, FAR, 1, 4, 3), 0, 9, 2),
+        (packed(1, 2, 3, FAR, 4), 1, 4, 4),
+        (packed(4, 1, 2, 3, FAR), 0, 9, 2),
+        (packed(1, 4, 3, 2, FAR), 1, 1, 3),
+        (packed(2, 1, 4, 3, FAR), 0, 9, 2),
+        (packed(1, 2, 3, 4, FAR), 1, 3, 4),
+    )
+    role = 2 * side + core + 4 * (1 - jnp.minimum(lax.rem(outer, 8), 1))
+
+    def planned(column):
+        value = jnp.int32(plans[0][column])
+        for at in range(1, len(plans)):
+            value = jnp.where(role == at, plans[at][column], value)
+        return value
+
+    order, pass2_at, pass4_at, merge_at = (planned(column) for column in range(4))
 
     def step(at_step, rest):
         slot, rest = lax.rem(rest, 8), rest // 8
@@ -295,20 +338,20 @@
             copy.start()
             copy.wait()
 
-        @pl.when((at_step == 1) & (core == 1))
+        @pl.when(at_step == pass4_at)
         def _():
             put4.wait_recv()
             put3.start()
 
-        @pl.when(at_step == 3 - soon)
+        @pl.when(at_step == pass2_at)
         def _():
             put2.wait_recv()
 
-        @pl.when((at_step == 3 - soon) & (core == 0))
+        @pl.when((at_step == pass2_at) & (core == 0))
         def _():
             put3.start()
 
-        @pl.when((at_step == 3 - soon) & (core == 1))
+        @pl.when((at_step == pass2_at) & (core == 1))
         def _():
             put1.start()
 
@@ -341,13 +384,13 @@
             def _():
                 term_put[sent].start()
 
-        @pl.when((slot == 2) & (core == 0))
+        @pl.when((at_step == merge_at) & (core == 0))
         def _():
             term_put[3].wait_recv()
             merge(2, 3)
             term_put[2].start()
 
-        @pl.when((slot == 3) & (core == 1))
+        @pl.when((at_step == merge_at) & (core == 1))
         def _():
             term_put[1].wait_recv()
             merge(2, 1)
@@ -355,27 +398,15 @@
 
         return rest
 
-    def packed(*order):
-        return sum(slot * 8**at for at, slot in enumerate(order))
-
-    orders = (
-        (packed(4, FAR, 3, 1, 2), packed(4, 3, 1, 2, FAR)),
-        (packed(1, 4, FAR, 2, 3), packed(1, 4, 2, 3, FAR)),
-    )
-    even, odd = (late * (1 - soon) + ahead * soon for late, ahead in orders)
-    lax.fori_loop(0, FAR, step, even * (1 - core) + odd * core)
+    lax.fori_loop(0, FAR, step, order)
 
     in_order = first < n_outer * n_inner
-    dq_out = []
     for half in range(2):
         rank = jnp.where(in_order, half, 1 - half)
         rows = pl.ds(half * span, span)
         dq = (dqt[rank] * scale).T.astype(BF16)
         for h in range(heads):
-            o_vm[rows, pl.ds(h * width, width)] = dq[h * span : (h + 1) * span]
-        copy = pltpu.make_async_copy(o_vm.at[rows, :], dq_ref.at[rows, :], kv_sem.at[0, half])
-        copy.start()
-        dq_out.append(copy)
+            dq_ref[rows, pl.ds(h * width, width)] = dq[h * span : (h + 1) * span]
 
     @pl.when(core == 0)
     def _():
@@ -397,24 +428,6 @@
 
     for copy in mark_puts + [put1, put2, put3, put4, put5] + list(term_put.values()):
         copy.wait_send()
-    for copy in dq_out:
-        copy.wait()
-
-
-def hand_over(dq, dk, dv, dq_out, dk_out, dv_out, dq_vm, dk_vm, dv_vm, sem):
-    rows = dq.shape[0] // 4
-    parts = [pl.ds(at * rows, rows) for at in range(4)]
-    routes = [(dq.at[part, :], dq_vm.at[part, :], dq_out.at[part, :]) for part in parts]
-    routes += [(dk, dk_vm, dk_out), (dv, dv_vm, dv_out)]
-    ins = [pltpu.make_async_copy(a, b, sem.at[0, at]) for at, (a, b, _) in enumerate(routes)]
-    outs = [pltpu.make_async_copy(b, c, sem.at[1, at]) for at, (_, b, c) in enumerate(routes)]
-    for copy in ins:
-        copy.start()
-    for came, goes in zip(ins, outs):
-        came.wait()
-        goes.start()
-    for copy in outs:
-        copy.wait()
 
 
 def shards(queries, keys, values, saved_out, saved_lse, out_grad, positions):
@@ -428,23 +441,15 @@
     stack = (2, heads * span, width)
     pair = (2, 2, span, width)
     dma = pltpu.SemaphoreType.DMA
-    results = pl.pallas_call(
+    return pl.pallas_call(
         functools.partial(kernel, lax.axis_size("outer"), lax.axis_size("inner")),
         out_shape=(
-            jax.ShapeDtypeStruct(queries.shape, BF16),
-            jax.ShapeDtypeStruct(keys.shape, BF16),
-            jax.ShapeDtypeStruct(values.shape, BF16),
+            pltpu.VMEM(queries.shape, BF16),
+            pltpu.VMEM(keys.shape, BF16),
+            pltpu.VMEM(values.shape, BF16),
         ),
-        in_specs=[
-            anywhere,
-            anywhere,
-            anywhere,
-            anywhere,
-            vmem,
-            anywhere,
-            pl.BlockSpec(memory_space=pltpu.SMEM),
-        ],
-        out_specs=[anywhere, vmem, vmem],
+        in_specs=[anywhere] * 7,
+        out_specs=[vmem] * 3,
         scratch_shapes=[
             pltpu.VMEM(stack, BF16),
             pltpu.VMEM(stack, BF16),
@@ -468,18 +473,14 @@
             dma((slots,)),
             dma((slots,)),
             pltpu.SemaphoreType.REGULAR,
+            pltpu.VMEM((heads, rows), F32),
+            pltpu.SMEM((rows,), jnp.int32),
+            dma((2,)),
         ],
         compiler_params=pltpu.CompilerParams(
             collective_id=0, has_side_effects=True, vmem_limit_bytes=56 * 2**20
         ),
     )(queries, keys, values, saved_out, saved_lse.T, out_grad, positions)
-    return pl.pallas_call(
-        hand_over,
-        out_shape=tuple(jax.ShapeDtypeStruct(x.shape, x.dtype) for x in results),
-        in_specs=[anywhere] * 3,
-        out_specs=[anywhere] * 3,
-        scratch_shapes=[pltpu.VMEM(x.shape, x.dtype) for x in results] + [dma((2, 6))],
-    )(*results)
 
 
 def solution(mesh):

time: 38 us -> 32.6 us (0.86)
  Pallas kernels: 37.2 us -> 29.7 us
  local copies, waits for them, and re-layouts: 0 us -> 2.16 us
    pallas_call x1, Pallas kernels: 35.1 us -> 29.7 us  [shards(): pl.pallas_call(functools.partial(kernel, lax.axis_size('outer'), lax.axis...]
    unnamed x0 -> x3, local copies, waits for them, and re-layouts: none -> 2.16 us
    pallas_call x1 -> x0, Pallas kernels: 2.06 us -> none  [shards(): pl.pallas_call(hand_over, out_shape=tuple((jax.ShapeDtypeStruct(x.shape,...]
where the time goes in v3:
time: 32.6 us; the launch traced here: 32.5 us
  Pallas kernels  29.7 us (91%)
  local copies, waits for them, and re-layouts  2.16 us (7%)
  between operations  0.64 us (2%)
    pallas_call x1, Pallas kernels, shards(): pl.pallas_call(functools.partial(kernel, lax.axis_size('outer'), lax.axis...  29.7 us
    unnamed x3, local copies, waits for them, and re-layouts  2.16 us

profile of v3, /device:TPU:224, one launch (start us, length us, event | category | flops | bytes accessed | tf_op | source)
XLA Modules:
  0.0 32.5 jit_solution(3222922671033921)
XLA Ops:
  0.6 29.7 %shard_map.94 = (bf16[384,1024]{1,0:T(8,128)(2,1)S(1)}, bf16[384,128]{1,0:T(8,128)(2,1)S(1)}, bf16[384,128]{1,0:T(8,128)(2,1)S(1)}) custom-call(bf16[384,1024]{1,0:T(8,128)(2,1)} %q_hbm.1, bf16[384,128]{1,0:T(8,128)(2,1)} %k_hbm.1, bf16[384,128]{1,0:T(8,128)(2,1)} %v_hbm.1, bf16[384,1024]{1,0:T(8,128)(2,1)} %o_hbm.1, f32[8,384]{1,0:T(8,128)} %bitcast.1, ...), custom_call_target="tpu_custom_call" | custom-call | tf_op jit(solution)/shard_map/pallas_call | solution.py:444
  30.3 0.9 %copy.13 = bf16[384,1024]{1,0:T(8,128)(2,1)} copy(bf16[384,1024]{1,0:T(8,128)(2,1)S(1)} %get-tuple-element.3) | data formatting | bytes 1572864
  31.2 0.6 %copy.14 = bf16[384,128]{1,0:T(8,128)(2,1)} copy(bf16[384,128]{1,0:T(8,128)(2,1)S(1)} %get-tuple-element.4) | data formatting | bytes 196608
  31.9 0.6 %copy.15 = bf16[384,128]{1,0:T(8,128)(2,1)} copy(bf16[384,128]{1,0:T(8,128)(2,1)S(1)} %get-tuple-element.5) | data formatting | bytes 196608

commit v4 on v3

--- a/solution.py
+++ b/solution.py
@@ -20,10 +20,6 @@
 
 def nt(a, b):
     return lax.dot_general(a, b, (((1,), (1,)), ((), ())), preferred_element_type=F32)
-
-
-def tn(a, b):
-    return lax.dot_general(a, b, (((0,), (0,)), ((), ())), preferred_element_type=F32)
 
 
 def kernel(
@@ -41,8 +37,7 @@
     dv_ref,
     qs,
     gs,
-    yq,
-    yg,
+    stats,
     o_vm,
     kv,
     mark,
@@ -177,7 +172,7 @@
     def _():
         put4.start()
 
-    @pl.when((side == 0) | (core == 0))
+    @pl.when(core == 0)
     def _():
         put2.start()
 
@@ -206,31 +201,19 @@
     pltpu.make_async_copy(gs, gs, load_sem.at[0]).wait()
     o_copy.wait()
     lane = lax.broadcasted_iota(jnp.int32, (span, width), 1)
-    spread = jnp.where(lane < 3 * heads, lax.rem(lane, heads), -1)
-
-    def split(x):
-        hi = x.astype(BF16).astype(F32)
-        mid = (x - hi).astype(BF16).astype(F32)
-        return jnp.where(lane < heads, hi, jnp.where(lane < 2 * heads, mid, x - hi - mid))
-
-    norm_rows = jnp.concatenate(
-        [lse_ref[...] * (1.0 / scale)] * 3 + [jnp.zeros((width - 3 * heads, 2 * span), F32)], 0
-    )
-    norm_table = norm_rows.T
+    dots = []
     for half in range(2):
-        rows = pl.ds(half * span, span)
-        dots = jnp.zeros((span, width), F32)
+        table = jnp.zeros((span, width), F32)
         for h in range(heads):
             g = gs[half, pl.ds(h * span, span), :].astype(F32)
-            o = o_vm[rows, pl.ds(h * width, width)].astype(F32)
-            dots = jnp.where(spread == h, jnp.sum(g * o, axis=1, keepdims=True), dots)
-        dots, norms = split(dots), split(norm_table[half * span : (half + 1) * span])
-        for h in range(heads):
-            to = pl.ds(h * span, span)
-            yg[half, to, :] = jnp.where(spread == h, dots, 0.0).astype(BF16)
-            yq[half, to, :] = jnp.where(spread == h, norms, 0.0).astype(BF16)
-
-    minus = jnp.where(lane < 3 * heads, -1.0, 0.0).astype(BF16)
+            o = o_vm[pl.ds(half * span, span), pl.ds(h * width, width)].astype(F32)
+            table = jnp.where(lane == h, jnp.sum(g * o, axis=1, keepdims=True), table)
+        dots.append(table)
+    tables = (lse_ref[...] * float(np.log2(np.e)), jnp.concatenate(dots, 0).T)
+    for at, table in enumerate(tables):
+        for half in range(2):
+            pieces = [table[h : h + 1, half * span : (half + 1) * span] for h in range(heads)]
+            stats[at, half] = jnp.concatenate(pieces, 1)
 
     columns = heads * span
     high = jnp.where(first < n_outer * n_inner, 1, 0)
@@ -239,16 +222,14 @@
     def unit(slot, key_half, query_half, diagonal):
         k, v = (lax.select(key_half == 1, kv[slot, at, 1], kv[slot, at, 0]) for at in range(2))
         q, g = qs[query_half], gs[query_half]
-        scores = nt(jnp.concatenate([k, minus], 1), jnp.concatenate([q, yq[query_half]], 1))
-        probs = jnp.exp2(scores * exp_scale)
+        probs = jnp.exp2(nt(k, q) * exp_scale - stats[0, query_half])
         if diagonal:
             t = lax.rem(lax.broadcasted_iota(jnp.int32, (1, columns), 1), span)
             u = lax.broadcasted_iota(jnp.int32, (span, 1), 0)
             probs = jnp.where(u <= t, probs, 0.0)
         probs_b = probs.astype(BF16)
-        shifted = nt(jnp.concatenate([v, minus], 1), jnp.concatenate([g, yg[query_half]], 1))
-        dscores = (probs * shifted).astype(BF16)
-        return nn(dscores, q), nn(probs_b, g), tn(k, dscores)
+        dscores = (probs * (nt(v, g) - stats[1, query_half])).astype(BF16)
+        return nn(dscores, q), nn(probs_b, g), nn(k.T, dscores)
 
     pltpu.make_async_copy(qs, qs, load_sem.at[1]).wait()
 
@@ -259,7 +240,7 @@
     def _():
         put4.start()
 
-    @pl.when((side == 1) & (core == 1))
+    @pl.when(core == 1)
     def _():
         put2.start()
 
@@ -271,18 +252,27 @@
     own[0, 0] += dk
     own[1, 0] += dv
     dqt[1] = dq
+    def mark_load_of(slot):
+        return pltpu.make_async_copy(marks.at[slot], mark_load.at[slot], mark_recv.at[slot])
+
+    def mark_in(slot):
+        mark_puts[slot - 1].wait_recv()
+        return mark_load_of(slot)
+
+    mark_loads = [mark_in(slot) for slot in range(1, REACH + 1)]
+    for copy in mark_loads:
+        copy.start()
+
+    far_late = lax.rem(outer, 8) < 2
+
+    @pl.when(jnp.logical_not(far_late))
+    def _():
+        mark_in(FAR).start()
+
     dk, dv, dq = unit(0, high, high, True)
     own[0, 1], own[1, 1] = dk, dv
     dqt[1] += dq
 
-    def mark_in(slot):
-        mark_puts[slot - 1].wait_recv()
-        return pltpu.make_async_copy(marks.at[slot], mark_load.at[slot], mark_recv.at[slot])
-
-    mark_loads = [mark_in(slot) for slot in range(1, REACH + 1)]
-    for copy in mark_loads:
-        copy.start()
-
     @pl.when(side == 1)
     def _():
         put4.start()
@@ -294,7 +284,11 @@
     for copy in mark_loads:
         copy.wait()
 
-    targets = {1: mate, 2: inner_at(-2), 3: inner_at(2 * core - 3), 4: inner_at(-4), FAR: outer_at(-1)}
+    @pl.when(jnp.logical_not(far_late))
+    def _():
+        mark_load_of(FAR).wait()
+
+    targets = {1: mate, 2: inner_at(-2), 3: inner_at((1 - core) * (1 - 4 * side) - core), 4: inner_at(-4), FAR: outer_at(-1)}
     term_put = {
         slot: remote(terms.at[slot], came.at[slot], term_send.at[slot], term_recv.at[slot], targets[slot])
         for slot in targets
@@ -310,16 +304,16 @@
         return sum(slot * 8**at for at, slot in enumerate(order))
 
     plans = (
-        (packed(4, 1, 2, FAR, 3), 0, 9, 2),
-        (packed(1, 4, 3, 2, FAR), 1, 1, 3),
-        (packed(2, FAR, 1, 4, 3), 0, 9, 2),
-        (packed(1, 2, 3, FAR, 4), 1, 4, 4),
-        (packed(4, 1, 2, 3, FAR), 0, 9, 2),
-        (packed(1, 4, 3, 2, FAR), 1, 1, 3),
-        (packed(2, 1, 4, 3, FAR), 0, 9, 2),
-        (packed(1, 2, 3, 4, FAR), 1, 3, 4),
+        (packed(4, 2, 3, 1, FAR), 0, 9, 2, 9),
+        (packed(1, 3, 4, 2, FAR), 2, 1, 4, 3),
+        (packed(2, FAR, 1, 4, 3), 0, 9, 2, 9),
+        (packed(1, 3, 2, FAR, 4), 2, 4, 3, 9),
+        (packed(4, 2, 3, 1, FAR), 0, 9, 2, 9),
+        (packed(1, 3, 4, 2, FAR), 2, 1, 4, 3),
+        (packed(2, 1, 4, 3, FAR), 0, 9, 2, 9),
+        (packed(1, 3, 2, 4, FAR), 1, 3, 3, 9),
     )
-    role = 2 * side + core + 4 * (1 - jnp.minimum(lax.rem(outer, 8), 1))
+    role = 2 * side + core + jnp.where(far_late, 4, 0)
 
     def planned(column):
         value = jnp.int32(plans[0][column])
@@ -327,12 +321,12 @@
             value = jnp.where(role == at, plans[at][column], value)
         return value
 
-    order, pass2_at, pass4_at, merge_at = (planned(column) for column in range(4))
+    order, pass2_at, pass4_at, merge2_at, merge4_at = (planned(column) for column in range(5))
 
     def step(at_step, rest):
         slot, rest = lax.rem(rest, 8), rest // 8
 
-        @pl.when(slot == FAR)
+        @pl.when((slot == FAR) & far_late)
         def _():
             copy = mark_in(FAR)
             copy.start()
@@ -378,19 +372,29 @@
             terms[slot, at, 0] = ((one + two_low) * factor).astype(BF16)
             terms[slot, at, 1] = ((two - two_low) * factor).astype(BF16)
 
-        for sent in (1, 3, 4, FAR):
+        for sent in (1, 3, FAR):
 
             @pl.when(slot == sent)
             def _():
                 term_put[sent].start()
 
-        @pl.when((at_step == merge_at) & (core == 0))
+        @pl.when((slot == 4) & ((side == 1) | (core == 0)))
+        def _():
+            term_put[4].start()
+
+        @pl.when(at_step == merge4_at)
+        def _():
+            term_put[3].wait_recv()
+            merge(4, 3)
+            term_put[4].start()
+
+        @pl.when((at_step == merge2_at) & (core == 0))
         def _():
             term_put[3].wait_recv()
             merge(2, 3)
             term_put[2].start()
 
-        @pl.when((at_step == merge_at) & (core == 1))
+        @pl.when((at_step == merge2_at) & (core == 1))
         def _():
             term_put[1].wait_recv()
             merge(2, 1)
@@ -412,17 +416,19 @@
     def _():
         term_put[1].wait_recv()
 
-    @pl.when(core == 1)
+    @pl.when((core == 1) & (side == 1))
     def _():
         term_put[3].wait_recv()
 
+    direct = jnp.where((core == 0) | (side == 1), 1.0, 0.0)
     for slot in (2, 4, FAR):
         term_put[slot].wait_recv()
     for at, out in enumerate((dk_ref, dv_ref)):
         for half in range(2):
             rank = jnp.where(in_order, half, 1 - half)
             total = own[at, rank] * (1.0 if at else scale)
-            for slot in (1 + 2 * core, 2, 4, FAR):
+            total += came[1 + 2 * core, at, rank].astype(F32) * direct
+            for slot in (2, 4, FAR):
                 total += came[slot, at, rank].astype(F32)
             out[pl.ds(half * span, span), :] = total.astype(BF16)
 
@@ -453,8 +459,7 @@
         scratch_shapes=[
             pltpu.VMEM(stack, BF16),
             pltpu.VMEM(stack, BF16),
-            pltpu.VMEM(stack, BF16),
-            pltpu.VMEM(stack, BF16),
+            pltpu.VMEM((2, 2, 1, heads * span), F32),
             pltpu.VMEM((rows, columns), BF16),
             pltpu.VMEM((slots,) + pair, BF16),
             pltpu.VMEM((8, 128), jnp.int32),

time: 32.6 us -> 30.4 us (0.933)
  Pallas kernels: 29.7 us -> 27.5 us
    pallas_call x1, Pallas kernels: 29.7 us -> 27.5 us  [shards(): pl.pallas_call(functools.partial(kernel, lax.axis_size('outer'), lax.axis...]
where the time goes in v4:
time: 30.4 us; the launch traced here: 30.3 us
  Pallas kernels  27.5 us (90%)
  local copies, waits for them, and re-layouts  2.16 us (7%)
  between operations  0.64 us (2%)
    pallas_call x1, Pallas kernels, shards(): pl.pallas_call(functools.partial(kernel, lax.axis_size('outer'), lax.axis...  27.5 us
    unnamed x3, local copies, waits for them, and re-layouts  2.16 us

profile of v4, /device:TPU:224, one launch (start us, length us, event | category | flops | bytes accessed | tf_op | source)
XLA Modules:
  0.0 30.3 jit_solution(773404920424622390)
XLA Ops:
  0.6 27.5 %shard_map.94 = (bf16[384,1024]{1,0:T(8,128)(2,1)S(1)}, bf16[384,128]{1,0:T(8,128)(2,1)S(1)}, bf16[384,128]{1,0:T(8,128)(2,1)S(1)}) custom-call(bf16[384,1024]{1,0:T(8,128)(2,1)} %q_hbm.1, bf16[384,128]{1,0:T(8,128)(2,1)} %k_hbm.1, bf16[384,128]{1,0:T(8,128)(2,1)} %v_hbm.1, bf16[384,1024]{1,0:T(8,128)(2,1)} %o_hbm.1, f32[8,384]{1,0:T(8,128)} %bitcast.1, ...), custom_call_target="tpu_custom_call" | custom-call | tf_op jit(solution)/shard_map/pallas_call | solution.py:450
  28.1 0.9 %copy.13 = bf16[384,1024]{1,0:T(8,128)(2,1)} copy(bf16[384,1024]{1,0:T(8,128)(2,1)S(1)} %get-tuple-element.3) | data formatting | bytes 1572864
  29.0 0.6 %copy.14 = bf16[384,128]{1,0:T(8,128)(2,1)} copy(bf16[384,128]{1,0:T(8,128)(2,1)S(1)} %get-tuple-element.4) | data formatting | bytes 196608
  29.6 0.6 %copy.15 = bf16[384,128]{1,0:T(8,128)(2,1)} copy(bf16[384,128]{1,0:T(8,128)(2,1)S(1)} %get-tuple-element.5) | data formatting | bytes 196608

commit v5 on v4

--- a/solution.py
+++ b/solution.py
@@ -32,9 +32,7 @@
     lse_hbm,
     g_hbm,
     pos_hbm,
-    dq_ref,
-    dk_ref,
-    dv_ref,
+    out_ref,
     qs,
     gs,
     stats,
@@ -177,6 +175,7 @@
         put2.start()
 
     early = lax.rem(outer, 8) == 0
+    last = lax.rem(outer, 8) == 7
 
     def reach_outer():
         @pl.when(core == 1)
@@ -190,7 +189,7 @@
 
         mark_puts[REACH].start()
 
-        @pl.when(early | (core == 0))
+        @pl.when(early | last | (core == 0))
         def _():
             put5.start()
 
@@ -244,7 +243,7 @@
     def _():
         put2.start()
 
-    @pl.when(jnp.logical_not(early) & (core == 1))
+    @pl.when(jnp.logical_not(early | last) & (core == 1))
     def _():
         put5.start()
 
@@ -252,6 +251,11 @@
     own[0, 0] += dk
     own[1, 0] += dv
     dqt[1] = dq
+
+    @pl.when(side == 1)
+    def _():
+        put4.start()
+
     def mark_load_of(slot):
         return pltpu.make_async_copy(marks.at[slot], mark_load.at[slot], mark_recv.at[slot])
 
@@ -273,9 +277,6 @@
     own[0, 1], own[1, 1] = dk, dv
     dqt[1] += dq
 
-    @pl.when(side == 1)
-    def _():
-        put4.start()
 
     @pl.when(early)
     def _():
@@ -305,15 +306,19 @@
 
     plans = (
         (packed(4, 2, 3, 1, FAR), 0, 9, 2, 9),
-        (packed(1, 3, 4, 2, FAR), 2, 1, 4, 3),
+        (packed(1, 3, FAR, 4, 2), 2, 1, 4, 3),
         (packed(2, FAR, 1, 4, 3), 0, 9, 2, 9),
         (packed(1, 3, 2, FAR, 4), 2, 4, 3, 9),
         (packed(4, 2, 3, 1, FAR), 0, 9, 2, 9),
         (packed(1, 3, 4, 2, FAR), 2, 1, 4, 3),
         (packed(2, 1, 4, 3, FAR), 0, 9, 2, 9),
         (packed(1, 3, 2, 4, FAR), 1, 3, 3, 9),
+        (packed(4, 2, 3, FAR, 1), 0, 9, 2, 9),
+        (packed(1, 3, FAR, 4, 2), 2, 1, 4, 3),
+        (packed(2, 1, FAR, 4, 3), 0, 9, 2, 9),
+        (packed(1, 3, 2, FAR, 4), 2, 4, 3, 9),
     )
-    role = 2 * side + core + jnp.where(far_late, 4, 0)
+    role = 2 * side + core + jnp.where(early, 4, 0) + jnp.where(lax.rem(outer, 8) == 1, 8, 0)
 
     def planned(column):
         value = jnp.int32(plans[0][column])
@@ -410,7 +415,7 @@
         rows = pl.ds(half * span, span)
         dq = (dqt[rank] * scale).T.astype(BF16)
         for h in range(heads):
-            dq_ref[rows, pl.ds(h * width, width)] = dq[h * span : (h + 1) * span]
+            out_ref[rows, pl.ds(h * width, width)] = dq[h * span : (h + 1) * span]
 
     @pl.when(core == 0)
     def _():
@@ -423,14 +428,14 @@
     direct = jnp.where((core == 0) | (side == 1), 1.0, 0.0)
     for slot in (2, 4, FAR):
         term_put[slot].wait_recv()
-    for at, out in enumerate((dk_ref, dv_ref)):
+    for at in range(2):
         for half in range(2):
             rank = jnp.where(in_order, half, 1 - half)
             total = own[at, rank] * (1.0 if at else scale)
             total += came[1 + 2 * core, at, rank].astype(F32) * direct
             for slot in (2, 4, FAR):
                 total += came[slot, at, rank].astype(F32)
-            out[pl.ds(half * span, span), :] = total.astype(BF16)
+            out_ref[pl.ds(half * span, span), pl.ds((heads + at) * width, width)] = total.astype(BF16)
 
     for copy in mark_puts + [put1, put2, put3, put4, put5] + list(term_put.values()):
         copy.wait_send()
@@ -447,15 +452,11 @@
     stack = (2, heads * span, width)
     pair = (2, 2, span, width)
     dma = pltpu.SemaphoreType.DMA
-    return pl.pallas_call(
+    grads = pl.pallas_call(
         functools.partial(kernel, lax.axis_size("outer"), lax.axis_size("inner")),
-        out_shape=(
-            pltpu.VMEM(queries.shape, BF16),
-            pltpu.VMEM(keys.shape, BF16),
-            pltpu.VMEM(values.shape, BF16),
-        ),
+        out_shape=pltpu.VMEM((rows, columns + 2 * width), BF16),
         in_specs=[anywhere] * 7,
-        out_specs=[vmem] * 3,
+        out_specs=vmem,
         scratch_shapes=[
             pltpu.VMEM(stack, BF16),
             pltpu.VMEM(stack, BF16),
@@ -486,6 +487,7 @@
             collective_id=0, has_side_effects=True, vmem_limit_bytes=56 * 2**20
         ),
     )(queries, keys, values, saved_out, saved_lse.T, out_grad, positions)
+    return grads[:, :columns], grads[:, columns : columns + width], grads[:, columns + width :]
 
 
 def solution(mesh):

time: 30.4 us -> 30 us (0.987)
  local copies, waits for them, and re-layouts: 2.16 us -> 1.67 us
    unnamed x3 -> x0, local copies, waits for them, and re-layouts: 2.16 us -> none
    slice x0 -> x2, local copies, waits for them, and re-layouts: none -> 1.67 us  [the longest x1 0.98 us: shards(): grads[:, :columns]]
where the time goes in v5:
time: 30 us; the launch traced here: 29.9 us
  Pallas kernels  27.6 us (92%)
  local copies, waits for them, and re-layouts  1.67 us (6%)
  between operations  0.64 us (2%)
    pallas_call x1, Pallas kernels, shards(): pl.pallas_call(functools.partial(kernel, lax.axis_size('outer'), lax.axis...  27.6 us
    slice x1, local copies, waits for them, and re-layouts, shards(): grads[:, :columns]  0.98 us
    slice x1, local copies, waits for them, and re-layouts, shards(): grads[:, columns + width:]  0.69 us

profile of v5, /device:TPU:224, one launch (start us, length us, event | category | flops | bytes accessed | tf_op | source)
XLA Modules:
  0.0 29.9 jit_solution(15958528904756485117)
XLA Ops:
  0.6 27.6 %shard_map.94 = bf16[384,1280]{1,0:T(8,128)(2,1)S(1)} custom-call(bf16[384,1024]{1,0:T(8,128)(2,1)} %q_hbm.1, bf16[384,128]{1,0:T(8,128)(2,1)} %k_hbm.1, bf16[384,128]{1,0:T(8,128)(2,1)} %v_hbm.1, bf16[384,1024]{1,0:T(8,128)(2,1)} %o_hbm.1, f32[8,384]{1,0:T(8,128)} %bitcast.1, bf16[384,1024]{1,0:T(8,128)(2,1)} %g_hbm.1, s32[384]{0:T(512)} %pos_hbm.1), custom_call_target="tpu_custom_call" | custom-call | tf_op jit(solution)/shard_map/pallas_call | solution.py:455
  28.2 0.7 %fusion = (bf16[384,128]{1,0:T(8,128)(2,1)}, bf16[384,128]{1,0:T(8,128)(2,1)}) fusion(bf16[384,1280]{1,0:T(8,128)(2,1)S(1)} %shard_map.94), kind=kLoop, calls=%fused_computation | loop fusion | bytes 393216 | tf_op jit(solution)/shard_map/slice | solution.py:490
  28.9 1.0 %slice.9 = bf16[384,1024]{1,0:T(8,128)(2,1)} slice(bf16[384,1280]{1,0:T(8,128)(2,1)S(1)} %shard_map.94), slice={[0:384], [0:1024]} | slice | bytes 1572864 | tf_op jit(solution)/shard_map/slice | solution.py:490

commit v6 on v5

--- a/solution.py
+++ b/solution.py
@@ -175,7 +175,6 @@
         put2.start()
 
     early = lax.rem(outer, 8) == 0
-    last = lax.rem(outer, 8) == 7
 
     def reach_outer():
         @pl.when(core == 1)
@@ -189,7 +188,7 @@
 
         mark_puts[REACH].start()
 
-        @pl.when(early | last | (core == 0))
+        @pl.when(early | (core == 0))
         def _():
             put5.start()
 
@@ -243,7 +242,7 @@
     def _():
         put2.start()
 
-    @pl.when(jnp.logical_not(early | last) & (core == 1))
+    @pl.when(jnp.logical_not(early) & (core == 1))
     def _():
         put5.start()
 
@@ -309,10 +308,10 @@
         (packed(1, 3, FAR, 4, 2), 2, 1, 4, 3),
         (packed(2, FAR, 1, 4, 3), 0, 9, 2, 9),
         (packed(1, 3, 2, FAR, 4), 2, 4, 3, 9),
-        (packed(4, 2, 3, 1, FAR), 0, 9, 2, 9),
+        (packed(4, 2, 3, 1, FAR), 0, 9, 4, 9),
         (packed(1, 3, 4, 2, FAR), 2, 1, 4, 3),
-        (packed(2, 1, 4, 3, FAR), 0, 9, 2, 9),
-        (packed(1, 3, 2, 4, FAR), 1, 3, 3, 9),
+        (packed(2, 1, 4, 3, FAR), 0, 9, 4, 9),
+        (packed(1, 3, 2, 4, FAR), 1, 3, 4, 9),
         (packed(4, 2, 3, FAR, 1), 0, 9, 2, 9),
         (packed(1, 3, FAR, 4, 2), 2, 1, 4, 3),
         (packed(2, 1, FAR, 4, 3), 0, 9, 2, 9),

time: 30 us -> 29.9 us (level)
  no operation moved by 1% of the time
where the time goes in v6:
time: 29.9 us; the launch traced here: 29.8 us
  Pallas kernels  27.5 us (92%)
  local copies, waits for them, and re-layouts  1.67 us (6%)
  between operations  0.64 us (2%)
    pallas_call x1, Pallas kernels, shards(): pl.pallas_call(functools.partial(kernel, lax.axis_size('outer'), lax.axis...  27.5 us
    slice x1, local copies, waits for them, and re-layouts, shards(): grads[:, :columns]  0.98 us
    slice x1, local copies, waits for them, and re-layouts, shards(): grads[:, columns + width:]  0.69 us

profile of v6, /device:TPU:224, one launch (start us, length us, event | category | flops | bytes accessed | tf_op | source)
XLA Modules:
  0.0 29.8 jit_solution(14775810557235650817)
XLA Ops:
  0.6 27.5 %shard_map.94 = bf16[384,1280]{1,0:T(8,128)(2,1)S(1)} custom-call(bf16[384,1024]{1,0:T(8,128)(2,1)} %q_hbm.1, bf16[384,128]{1,0:T(8,128)(2,1)} %k_hbm.1, bf16[384,128]{1,0:T(8,128)(2,1)} %v_hbm.1, bf16[384,1024]{1,0:T(8,128)(2,1)} %o_hbm.1, f32[8,384]{1,0:T(8,128)} %bitcast.1, bf16[384,1024]{1,0:T(8,128)(2,1)} %g_hbm.1, s32[384]{0:T(512)} %pos_hbm.1), custom_call_target="tpu_custom_call" | custom-call | tf_op jit(solution)/shard_map/pallas_call | solution.py:454
  28.2 0.7 %fusion = (bf16[384,128]{1,0:T(8,128)(2,1)}, bf16[384,128]{1,0:T(8,128)(2,1)}) fusion(bf16[384,1280]{1,0:T(8,128)(2,1)S(1)} %shard_map.94), kind=kLoop, calls=%fused_computation | loop fusion | bytes 393216 | tf_op jit(solution)/shard_map/slice | solution.py:489
  28.8 1.0 %slice.9 = bf16[384,1024]{1,0:T(8,128)(2,1)} slice(bf16[384,1280]{1,0:T(8,128)(2,1)S(1)} %shard_map.94), slice={[0:384], [0:1024]} | slice | bytes 1572864 | tf_op jit(solution)/shard_map/slice | solution.py:489
